TPU v7x, 512 devices: a whole 4x8x8 slice. The times are simulated.
512 devices in a mesh: row: 64 (over z, x, core), col: 8 (over y).
Axes of the slice: x: 4, y: 8, z: 8, core: 2. Of those that a mesh axis runs over, the one named last changes fastest.
Arguments:
- front_in: float32 [32768, 4096], P('row', 'col')
- child_block: float32 [32768, 2048], P('row', 'col'), may hold values from -6 to 6
- child_rows: int32 [32768], P('row'), may hold values from 0 to 32767, as said below
- live_counts: int32 [64, 64], P('row'), may hold values from 0 to 8, as said below
- column_map: int32 [2048], P('col'), may hold values from 0 to 4095, as said below
Outputs:
- parent_front: float32 [32768, 4096], P('row', 'col')
- factor_rows: float32 [512, 4096], P(None, 'col')
Inputs may be any that keep to these rules, and one draw needn't show every extreme that they name: `child_rows`: child row i of each row block (0 <= i < 512) goes to a parent row of row block i // 8, that is into rows (i // 8) * 512 to (i // 8 + 1) * 512 - 1; parent rows may repeat. Each row of live_counts holds both 0 and 8. `column_map`: the child columns held by column block c map to distinct parent columns of the same block, c * 512 to (c + 1) * 512 - 1.
All inputs are finite; a program needn't handle non-finite values.
Results may differ from a plain program's by a relative error of at most 0.00029.
Values sent between devices are 32-bit elements; how exact they have to be, the bound alone decides.
No kernel may reach another device: no remote copies, remote signals or barrier semaphores. Data moves between devices by JAX's collectives and lax.ppermute only.
A program may use at most 64 MiB of HBM per device.

v0:
```python
import math
import jax
import jax.numpy as jnp
from jax import lax
from jax.sharding import PartitionSpec as P

PANEL = 256


def swapped(shard, axis, apart):
    return lax.ppermute(shard, axis, [(i, i ^ 1 << apart) for i in range(lax.axis_size(axis))])


def from_root(shard, axis, root):
    mine = lax.axis_index(axis) == root
    return lax.psum(jnp.where(mine, shard, jnp.zeros_like(shard)), axis)


def factor_panel(panel_cols, highest):
    gram_matrix = jnp.dot(panel_cols.T, panel_cols, precision=highest)
    for bit_index in range(lax.axis_size("row").bit_length() - 1):
        partner = swapped(gram_matrix, "row", bit_index)
        gram_matrix = gram_matrix + partner
    upper_factor = jnp.linalg.cholesky(gram_matrix).T
    basis_cols = jax.scipy.linalg.solve_triangular(upper_factor.T, panel_cols.T, lower=True).T
    return (upper_factor, basis_cols)


def on_device(front_in, child_block, child_rows, live_counts, column_map):
    highest = lax.Precision.HIGHEST
    rows_dev, cols_dev = front_in.shape
    owners = lax.axis_size("row")
    capacity = child_block.shape[0] // owners
    child_width = child_block.shape[1]
    slot_index = jnp.arange(capacity, dtype=jnp.int32)
    live_mask = (slot_index[None, :] < live_counts[0][:, None]).astype(jnp.float32)
    payload = child_block.reshape(owners, capacity, child_width) * live_mask[:, :, None]
    targets = child_rows.reshape(owners, capacity)
    arrived, arrived_rows = (
        lax.all_to_all(payload, "row", split_axis=0, concat_axis=0, tiled=True),
        lax.all_to_all(targets, "row", split_axis=0, concat_axis=0, tiled=True),
    )
    local_cols = column_map % cols_dev
    one_hot = (local_cols[:, None] == jnp.arange(cols_dev, dtype=jnp.int32)[None, :]).astype(
        jnp.float32
    )
    placed = jnp.dot(arrived.reshape(owners * capacity, child_width), one_hot, precision=highest)
    parent_front = front_in.at[arrived_rows.reshape(owners * capacity) % rows_dev].add(placed)
    global_cols = lax.axis_index("col") * cols_dev + jnp.arange(cols_dev, dtype=jnp.int32)
    root_rows = math.sqrt(rows_dev * owners)
    blocks = []
    for panel_index in range(2):
        first_col = panel_index * PANEL
        last_col = first_col + PANEL
        upper_factor, basis_cols = factor_panel(parent_front[:, first_col:last_col], highest)
        basis_cols = from_root(basis_cols, "col", 0)
        product = lax.psum(jnp.dot(basis_cols.T, parent_front, precision=highest), "row")
        trailing = (global_cols >= last_col)[None, :]
        in_panel = ((global_cols >= first_col) & (global_cols < last_col))[None, :]
        coupled = jnp.where(trailing, product, jnp.zeros_like(product))
        parent_front = parent_front - jnp.dot(basis_cols, coupled, precision=highest)
        widths = ((0, 0), (first_col, cols_dev - last_col))
        parent_front = jnp.where(in_panel, jnp.pad(basis_cols * root_rows, widths), parent_front)
        blocks.append(jnp.where(in_panel, jnp.pad(upper_factor, widths), coupled) / root_rows)
    return (parent_front, jnp.concatenate(blocks, axis=0))


def solution(mesh):
    return jax.shard_map(
        on_device,
        mesh=mesh,
        in_specs=(P("row", "col"), P("row", "col"), P("row"), P("row", None), P("col")),
        out_specs=(P("row", "col"), P(None, "col")),
        check_vma=False,
    )
```

profile of v0, /device:TPU:8, one launch (start us, length us, event | category | flops | bytes accessed | tf_op | source)
XLA Modules:
  0.0 877.8 jit_solution(3618747720132949880)
XLA Ops:
  7.2 0.7 copy-done.7
  8.6 13.8 %all-to-all-start = ((s32[64,1,8]{2,1,0:T(1,128)}), s32[64,1,8]{2,1,0:T(1,128)S(1)}, u32[]{:S(2)}, u32[]{:S(2)}) async-start(s32[64,1,8]{2,1,0:T(1,128)} %bitcast), calls=%async_computation | async-start | bytes 65536 | tf_op jit(solution)/shard_map/all_to_all | solution.py:41
  23.2 0.9 bitcast_multiply_fusion
  24.1 7.9 all-to-all-done
  31.9 4.8 all-to-all-start.1
  37.4 0.8 reduce.11
  38.3 16.1 %all-to-all-done.1 = f32[64,8,256]{2,1,0:T(8,128)S(1)} async-done(((f32[64,8,256]{2,1,0:T(8,128)}), f32[64,8,256]{2,1,0:T(8,128)S(1)}, u32[]{:S(2)}, u32[]{:S(2)}) %all-to-all-start.1) | async-done | bytes 524320 | tf_op jit(solution)/shard_map/all_to_all | solution.py:40
  55.1 4.0 scatter_fusion
  59.1 1.0 fusion.53
  60.1 2.0 collective-permute-start
  62.1 1.4 collective-permute-done
  63.6 3.4 collective-permute-start.1
  67.0 6.8 collective-permute-done.1
  73.8 4.9 collective-permute-start.2
  78.7 6.0 collective-permute-done.2
  84.8 3.1 collective-permute-start.3
  87.9 5.4 collective-permute-done.3
  93.3 4.7 collective-permute-start.4
  98.0 9.5 %collective-permute-done.4 = f32[256,256]{0,1:T(8,128)S(1)} collective-permute-done((f32[256,256]{0,1:T(8,128)S(1)}, f32[256,256]{0,1:T(8,128)S(1)}, u32[]{:S(2)}, u32[]{:S(2)}) %collective-permute-start.4) | collective-permute-done | bytes 262176 | tf_op jit(solution)/shard_map/ppermute | solution.py:11
  107.6 4.8 collective-permute-start.5
  112.7 13.2 %collective-permute-done.5 = f32[256,256]{0,1:T(8,128)S(1)} collective-permute-done((f32[256,256]{0,1:T(8,128)S(1)}, f32[256,256]{0,1:T(8,128)S(1)}, u32[]{:S(2)}, u32[]{:S(2)}) %collective-permute-start.5) | collective-permute-done | bytes 262176 | tf_op jit(solution)/shard_map/ppermute | solution.py:11
  126.1 11.7 %cholesky.130 = f32[128,128]{1,0:T(8,128)S(1)} custom-call(f32[128,128]{1,0:T(8,128)S(1)} %cholesky.194), custom_call_target="Cholesky" | custom-call | tf_op jit(solution)/shard_map/jit(cholesky)/cholesky | solution.py:24
  137.9 9.8 %custom-call.13 = f32[1,128,128]{1,2,0:T(8,128)S(1)} custom-call(f32[1,128,128]{2,1,0:T(8,128)S(1)} %get-tuple-element.57), custom_call_target="InvertDiagBlocksLowerTriangular" | custom-call | tf_op jit(solution)/shard_map/jit(cholesky)/cholesky | solution.py:24
  148.4 11.7 %cholesky.147 = f32[128,128]{1,0:T(8,128)S(1)} custom-call(f32[128,128]{1,0:T(8,128)S(1)} %slice_subtract_fusion.1), custom_call_target="Cholesky" | custom-call | tf_op jit(solution)/shard_map/jit(cholesky)/cholesky | solution.py:24
  162.3 4.4 while.4
  163.2 1.4 bitcast_dynamic-update-slice_fusion.4
  165.3 1.4 bitcast_dynamic-update-slice_fusion.4
  166.7 19.7 %custom-call.14 = f32[2,128,128]{1,2,0:T(8,128)S(1)} custom-call(f32[2,128,128]{2,1,0:T(8,128)S(1)} %get-tuple-element.18), custom_call_target="InvertDiagBlocksLowerTriangular" | custom-call | tf_op jit(solution)/shard_map/jit(_solve_triangular)/triangular_solve | solution.py:25
  187.9 0.8 fusion.2
  188.8 75.5 %all-reduce.10.cloned.1.call-done = f32[512,256]{1,0:T(8,128)} async-done(((f32[512,256]{1,0:T(8,128)}), f32[512,256]{1,0:T(8,128)}) %all-reduce.10.cloned.1.call-update) | async-done | bytes 524304 | tf_op jit(solution)/shard_map/psum | solution.py:16
  264.3 3.6 fusion.57
  268.1 1.0 copy-done.2
  269.1 191.8 %all-reduce.12.cloned.1.call-done = f32[256,512]{0,1:T(8,128)} async-done(((f32[256,512]{0,1:T(8,128)}), f32[256,512]{0,1:T(8,128)}) %all-reduce.12.cloned.1.call-update) | async-done | bytes 524304 | tf_op jit(solution)/shard_map/psum | solution.py:57
  460.9 2.2 fusion
  463.1 1.0 fusion.6
  464.1 1.9 collective-permute-start.6
  466.0 1.5 collective-permute-done.6
  467.5 3.1 collective-permute-start.7
  470.6 7.1 collective-permute-done.7
  477.8 4.4 collective-permute-start.8
  482.2 6.5 collective-permute-done.8
  488.8 1.9 collective-permute-start.9
  490.7 6.6 collective-permute-done.9
  497.3 3.4 collective-permute-start.10
  500.7 10.6 %collective-permute-done.10 = f32[256,256]{0,1:T(8,128)S(1)} collective-permute-done((f32[256,256]{0,1:T(8,128)S(1)}, f32[256,256]{0,1:T(8,128)S(1)}, u32[]{:S(2)}, u32[]{:S(2)}) %collective-permute-start.10) | collective-permute-done | bytes 262176 | tf_op jit(solution)/shard_map/ppermute | solution.py:11
  511.4 4.7 collective-permute-start.11
  516.2 13.5 %collective-permute-done.11 = f32[256,256]{0,1:T(8,128)S(1)} collective-permute-done((f32[256,256]{0,1:T(8,128)S(1)}, f32[256,256]{0,1:T(8,128)S(1)}, u32[]{:S(2)}, u32[]{:S(2)}) %collective-permute-start.11) | collective-permute-done | bytes 262176 | tf_op jit(solution)/shard_map/ppermute | solution.py:11
  530.0 11.7 %cholesky.164 = f32[128,128]{1,0:T(8,128)S(1)} custom-call(f32[128,128]{1,0:T(8,128)S(1)} %cholesky.197), custom_call_target="Cholesky" | custom-call | tf_op jit(solution)/shard_map/jit(cholesky)/cholesky | solution.py:24
  541.7 9.8 %custom-call.15 = f32[1,128,128]{1,2,0:T(8,128)S(1)} custom-call(f32[1,128,128]{2,1,0:T(8,128)S(1)} %get-tuple-element.53), custom_call_target="InvertDiagBlocksLowerTriangular" | custom-call | tf_op jit(solution)/shard_map/jit(cholesky)/cholesky | solution.py:24
  552.2 11.7 %cholesky.181 = f32[128,128]{1,0:T(8,128)S(1)} custom-call(f32[128,128]{1,0:T(8,128)S(1)} %slice_subtract_fusion), custom_call_target="Cholesky" | custom-call | tf_op jit(solution)/shard_map/jit(cholesky)/cholesky | solution.py:24
  566.7 4.1 while.5
  567.4 1.4 bitcast_dynamic-update-slice_fusion.5
  569.4 1.4 bitcast_dynamic-update-slice_fusion.5
  570.8 19.7 %custom-call.16 = f32[2,128,128]{1,2,0:T(8,128)S(1)} custom-call(f32[2,128,128]{2,1,0:T(8,128)S(1)} %get-tuple-element.19), custom_call_target="InvertDiagBlocksLowerTriangular" | custom-call | tf_op jit(solution)/shard_map/jit(_solve_triangular)/triangular_solve | solution.py:25
  592.0 0.8 fusion.3
  592.9 76.2 %all-reduce.14.cloned.1.call-done = f32[512,256]{1,0:T(8,128)} async-done(((f32[512,256]{1,0:T(8,128)}), f32[512,256]{1,0:T(8,128)}) %all-reduce.14.cloned.1.call-update) | async-done | bytes 524304 | tf_op jit(solution)/shard_map/psum | solution.py:16
  669.2 3.6 fusion.58
  672.8 1.0 copy-done.3
  673.9 1.0 select_multiply_fusion.1
  674.9 0.9 broadcast_multiply_fusion
  675.8 189.4 %all-reduce.16.cloned.1.call-done = f32[256,512]{0,1:T(8,128)} async-done(((f32[256,512]{0,1:T(8,128)}), f32[256,512]{0,1:T(8,128)}) %all-reduce.16.cloned.1.call-update) | async-done | bytes 524304 | tf_op jit(solution)/shard_map/psum | solution.py:57
  865.2 1.3 select_multiply_fusion
  866.6 1.3 copy.54
  868.0 3.1 fusion.1
  (97 shorter events, 13.6 us)
Async XLA Ops:
  7.2 16.0 %copy-start.6 = (f32[512,256]{1,0:T(8,128)S(1)}, f32[512,256]{1,0:T(8,128)}, u32[]{:S(2)}) copy-start(f32[512,256]{1,0:T(8,128)} %param.9) | copy-start | bytes 1572868
  7.2 0.7 copy-start.7
  8.6 23.3 %all-to-all-start = ((s32[64,1,8]{2,1,0:T(1,128)}), s32[64,1,8]{2,1,0:T(1,128)S(1)}, u32[]{:S(2)}, u32[]{:S(2)}) async-start(s32[64,1,8]{2,1,0:T(1,128)} %bitcast), calls=%async_computation | async-start | bytes 65536 | tf_op jit(solution)/shard_map/all_to_all | solution.py:41
  22.4 0.7 copy-start.9
  31.9 4.8 copy-start.8
  31.9 22.4 %all-to-all-start.1 = ((f32[64,8,256]{2,1,0:T(8,128)}), f32[64,8,256]{2,1,0:T(8,128)S(1)}, u32[]{:S(2)}, u32[]{:S(2)}) async-start(f32[64,8,256]{2,1,0:T(8,128)} %bitcast_multiply_fusion), calls=%async_computation.1 | async-start | bytes 1048576 | tf_op jit(solution)/shard_map/all_to_all | solution.py:40
  36.7 18.4 %copy-start = (f32[512,512]{1,0:T(8,128)S(1)}, f32[512,512]{1,0:T(8,128)}, u32[]{:S(2)}) copy-start(f32[512,512]{1,0:T(8,128)} %param.8) | copy-start | bytes 3145732
  36.7 227.6 %all-reduce.10.cloned.1.call-start = ((), (), s32[]{:S(2)}) async-start(), calls=%async_computation.2 | async-start | bytes 1048576 | tf_op jit(solution)/shard_map/psum | solution.py:16
  60.1 3.4 collective-permute-start
  63.6 10.2 %collective-permute-start.1 = (f32[256,256]{0,1:T(8,128)S(1)}, f32[256,256]{0,1:T(8,128)S(1)}, u32[]{:S(2)}, u32[]{:S(2)}) collective-permute-start(f32[256,256]{0,1:T(8,128)S(1)} %add.125), channel_id=1, source_target_pairs={{0,16},{8,24},{16,0},{24,8},{32,48},{40,56},{48,32},{56,40},{64,80... | collective-permute-start | bytes 786440 | tf_op jit(solution)/shard_map/ppermute | solution.py:11
  73.8 10.9 %collective-permute-start.2 = (f32[256,256]{0,1:T(8,128)S(1)}, f32[256,256]{0,1:T(8,128)S(1)}, u32[]{:S(2)}, u32[]{:S(2)}) collective-permute-start(f32[256,256]{0,1:T(8,128)S(1)} %add.126), channel_id=1, source_target_pairs={{0,32},{8,40},{16,48},{24,56},{32,0},{40,8},{48,16},{56,24},{64,96... | collective-permute-start | bytes 786440 | tf_op jit(solution)/shard_map/ppermute | solution.py:11
  84.8 8.5 collective-permute-start.3
  93.3 14.2 %collective-permute-start.4 = (f32[256,256]{0,1:T(8,128)S(1)}, f32[256,256]{0,1:T(8,128)S(1)}, u32[]{:S(2)}, u32[]{:S(2)}) collective-permute-start(f32[256,256]{0,1:T(8,128)S(1)} %add.128), channel_id=1, source_target_pairs={{0,128},{8,136},{16,144},{24,152},{32,160},{40,168},{48,176},{56,1... | collective-permute-start | bytes 786440 | tf_op jit(solution)/shard_map/ppermute | solution.py:11
  107.6 18.3 %collective-permute-start.5 = (f32[256,256]{0,1:T(8,128)S(1)}, f32[256,256]{0,1:T(8,128)S(1)}, u32[]{:S(2)}, u32[]{:S(2)}) collective-permute-start(f32[256,256]{0,1:T(8,128)S(1)} %add.129), channel_id=1, source_target_pairs={{0,256},{8,264},{16,272},{24,280},{32,288},{40,296},{48,304},{56,3... | collective-permute-start | bytes 786440 | tf_op jit(solution)/shard_map/ppermute | solution.py:11
  188.8 272.1 %all-reduce.12.cloned.1.call-start = ((), (), s32[]{:S(2)}) async-start(), calls=%async_computation.3 | async-start | bytes 1048576 | tf_op jit(solution)/shard_map/psum | solution.py:57
  268.0 1.0 copy-start.2
  268.0 401.1 %all-reduce.14.cloned.1.call-start = ((), (), s32[]{:S(2)}) async-start(), calls=%async_computation.4 | async-start | bytes 1048576 | tf_op jit(solution)/shard_map/psum | solution.py:16
  464.1 3.4 collective-permute-start.6
  467.5 10.2 %collective-permute-start.7 = (f32[256,256]{0,1:T(8,128)S(1)}, f32[256,256]{0,1:T(8,128)S(1)}, u32[]{:S(2)}, u32[]{:S(2)}) collective-permute-start(f32[256,256]{0,1:T(8,128)S(1)} %add.131), channel_id=1, source_target_pairs={{0,16},{8,24},{16,0},{24,8},{32,48},{40,56},{48,32},{56,40},{64,80... | collective-permute-start | bytes 786440 | tf_op jit(solution)/shard_map/ppermute | solution.py:11
  477.8 10.9 %collective-permute-start.8 = (f32[256,256]{0,1:T(8,128)S(1)}, f32[256,256]{0,1:T(8,128)S(1)}, u32[]{:S(2)}, u32[]{:S(2)}) collective-permute-start(f32[256,256]{0,1:T(8,128)S(1)} %add.132), channel_id=1, source_target_pairs={{0,32},{8,40},{16,48},{24,56},{32,0},{40,8},{48,16},{56,24},{64,96... | collective-permute-start | bytes 786440 | tf_op jit(solution)/shard_map/ppermute | solution.py:11
  488.8 8.5 collective-permute-start.9
  497.3 14.1 %collective-permute-start.10 = (f32[256,256]{0,1:T(8,128)S(1)}, f32[256,256]{0,1:T(8,128)S(1)}, u32[]{:S(2)}, u32[]{:S(2)}) collective-permute-start(f32[256,256]{0,1:T(8,128)S(1)} %add.134), channel_id=1, source_target_pairs={{0,128},{8,136},{16,144},{24,152},{32,160},{40,168},{48,176},{56,1... | collective-permute-start | bytes 786440 | tf_op jit(solution)/shard_map/ppermute | solution.py:11
  511.4 18.3 %collective-permute-start.11 = (f32[256,256]{0,1:T(8,128)S(1)}, f32[256,256]{0,1:T(8,128)S(1)}, u32[]{:S(2)}, u32[]{:S(2)}) collective-permute-start(f32[256,256]{0,1:T(8,128)S(1)} %add.135), channel_id=1, source_target_pairs={{0,256},{8,264},{16,272},{24,280},{32,288},{40,296},{48,304},{56,3... | collective-permute-start | bytes 786440 | tf_op jit(solution)/shard_map/ppermute | solution.py:11
  592.9 272.3 %all-reduce.16.cloned.1.call-start = ((), (), s32[]{:S(2)}) async-start(), calls=%async_computation.5 | async-start | bytes 1048576 | tf_op jit(solution)/shard_map/psum | solution.py:57
  672.8 1.0 copy-start.3
  673.9 1.0 copy-start.1
  865.2 1.3 copy-start.5
  866.6 1.3 copy-start.4
Sparse Core Ops, SparseCore 0:
  188.9 75.4 all-reduce.9
  268.8 192.0 all-reduce.11
  593.0 76.1 all-reduce.13
  673.1 192.0 all-reduce.15
where the time goes:
time: 884 us; the launch traced here: 878 us
  waiting for transfers between devices  645 us (73%)
  other arithmetic  119 us (13%)
  starting transfers between devices  61.1 us (7%)
  matrix products  19.2 us (2%)
  between operations  17.2 us (2%)
  local copies, waits for them, and re-layouts  15.2 us (2%)
    psum x2, waiting for transfers between devices, on_device(): lax.psum(jnp.dot(basis_cols.T, parent_front, precision=highest), 'row')  381 us
    psum x2, waiting for transfers between devices, from_root(): return lax.psum(jnp.where(mine, shard, jnp.zeros_like(shard)), axis)  152 us
    ppermute x12, waiting for transfers between devices, swapped(): lax.ppermute(shard, axis, [(i, i ^ 1 << apart) for i in range(lax.axis_si...  88.3 us
    another operation x13, other arithmetic, factor_panel(): upper_factor = jnp.linalg.cholesky(gram_matrix).T  68.6 us
    ppermute x12, starting transfers between devices, swapped(): lax.ppermute(shard, axis, [(i, i ^ 1 << apart) for i in range(lax.axis_si...  42.4 us
    another operation x3, other arithmetic, factor_panel(): jax.scipy.linalg.solve_triangular(upper_factor.T, panel_cols.T, lower=True)  39.4 us
  transfers between devices with their start and end apart: 18, of which 18 were waited for; matrix products, arithmetic and copies ran while one was open for 1% of the time, Pallas kernels for 0%

commit v1 on v0

--- a/solution.py
+++ b/solution.py
@@ -13,7 +13,7 @@
 
 def from_root(shard, axis, root):
     mine = lax.axis_index(axis) == root
-    return lax.psum(jnp.where(mine, shard, jnp.zeros_like(shard)), axis)
+    return jnp.sum(lax.all_gather(jnp.where(mine, shard, jnp.zeros_like(shard)), axis), axis=0)
 
 
 def factor_panel(panel_cols, highest):

time: 884 us -> 845 us (0.956)
  waiting for transfers between devices: 645 us -> 603 us
    psum x2 -> x0, waiting for transfers between devices: 152 us -> none  [from_root(): return lax.psum(jnp.where(mine, shard, jnp.zeros_like(shard)), axis)]
    all_gather x0 -> x2, waiting for transfers between devices: none -> 106 us  [from_root(): lax.all_gather(jnp.where(mine, shard, jnp.zeros_like(shard)), axis)]
where the time goes in v1:
time: 845 us; the launch traced here: 838 us
  waiting for transfers between devices  603 us (71%)
  other arithmetic  127 us (15%)
  starting transfers between devices  61 us (7%)
  matrix products  17.1 us (2%)
  between operations  17.1 us (2%)
  local copies, waits for them, and re-layouts  12.5 us (1%)
    psum x2, waiting for transfers between devices, on_device(): lax.psum(jnp.dot(basis_cols.T, parent_front, precision=highest), 'row')  386 us
    all_gather x2, waiting for transfers between devices, from_root(): lax.all_gather(jnp.where(mine, shard, jnp.zeros_like(shard)), axis)  106 us
    ppermute x12, waiting for transfers between devices, swapped(): lax.ppermute(shard, axis, [(i, i ^ 1 << apart) for i in range(lax.axis_si...  88.3 us
    another operation x13, other arithmetic, factor_panel(): upper_factor = jnp.linalg.cholesky(gram_matrix).T  68.7 us
    ppermute x12, starting transfers between devices, swapped(): lax.ppermute(shard, axis, [(i, i ^ 1 << apart) for i in range(lax.axis_si...  42.4 us
    another operation x3, other arithmetic, factor_panel(): jax.scipy.linalg.solve_triangular(upper_factor.T, panel_cols.T, lower=True)  39.4 us
  transfers between devices with their start and end apart: 18, of which 18 were waited for; matrix products, arithmetic and copies ran while one was open for 1% of the time, Pallas kernels for 0%

profile of v1, /device:TPU:8, one launch (start us, length us, event | category | flops | bytes accessed | tf_op | source)
XLA Modules:
  0.0 838.3 jit_solution(15495461223752232143)
XLA Ops:
  7.2 1.5 all_to_all.9
  8.7 13.8 %all-to-all-start = ((s32[64,1,8]{2,1,0:T(1,128)}), s32[64,1,8]{2,1,0:T(1,128)S(1)}, u32[]{:S(2)}, u32[]{:S(2)}) async-start(s32[64,1,8]{2,1,0:T(1,128)} %bitcast), calls=%async_computation | async-start | bytes 65536 | tf_op jit(solution)/shard_map/all_to_all | solution.py:41
  23.2 2.0 bitcast_multiply_fusion
  25.2 6.8 all-to-all-done
  32.0 4.6 all-to-all-start.1
  38.1 16.2 %all-to-all-done.1 = f32[64,8,256]{2,1,0:T(8,128)S(1)} async-done(((f32[64,8,256]{2,1,0:T(8,128)}), f32[64,8,256]{2,1,0:T(8,128)S(1)}, u32[]{:S(2)}, u32[]{:S(2)}) %all-to-all-start.1) | async-done | bytes 524320 | tf_op jit(solution)/shard_map/all_to_all | solution.py:40
  55.0 4.0 scatter_fusion
  59.0 1.0 fusion.53
  60.0 2.0 collective-permute-start
  62.0 1.4 collective-permute-done
  63.5 3.4 collective-permute-start.1
  66.9 6.8 collective-permute-done.1
  73.7 4.9 collective-permute-start.2
  78.6 6.0 collective-permute-done.2
  84.7 3.1 collective-permute-start.3
  87.8 5.4 collective-permute-done.3
  93.2 4.7 collective-permute-start.4
  97.9 9.5 %collective-permute-done.4 = f32[256,256]{0,1:T(8,128)S(1)} collective-permute-done((f32[256,256]{0,1:T(8,128)S(1)}, f32[256,256]{0,1:T(8,128)S(1)}, u32[]{:S(2)}, u32[]{:S(2)}) %collective-permute-start.4) | collective-permute-done | bytes 262176 | tf_op jit(solution)/shard_map/ppermute | solution.py:11
  107.5 4.8 collective-permute-start.5
  112.6 13.2 %collective-permute-done.5 = f32[256,256]{0,1:T(8,128)S(1)} collective-permute-done((f32[256,256]{0,1:T(8,128)S(1)}, f32[256,256]{0,1:T(8,128)S(1)}, u32[]{:S(2)}, u32[]{:S(2)}) %collective-permute-start.5) | collective-permute-done | bytes 262176 | tf_op jit(solution)/shard_map/ppermute | solution.py:11
  126.0 11.7 %cholesky.130 = f32[128,128]{1,0:T(8,128)S(1)} custom-call(f32[128,128]{1,0:T(8,128)S(1)} %cholesky.194), custom_call_target="Cholesky" | custom-call | tf_op jit(solution)/shard_map/jit(cholesky)/cholesky | solution.py:24
  137.8 9.8 %custom-call.13 = f32[1,128,128]{1,2,0:T(8,128)S(1)} custom-call(f32[1,128,128]{2,1,0:T(8,128)S(1)} %get-tuple-element.57), custom_call_target="InvertDiagBlocksLowerTriangular" | custom-call | tf_op jit(solution)/shard_map/jit(cholesky)/cholesky | solution.py:24
  148.3 11.7 %cholesky.147 = f32[128,128]{1,0:T(8,128)S(1)} custom-call(f32[128,128]{1,0:T(8,128)S(1)} %slice_subtract_fusion.1), custom_call_target="Cholesky" | custom-call | tf_op jit(solution)/shard_map/jit(cholesky)/cholesky | solution.py:24
  162.2 4.2 while.4
  163.0 1.3 bitcast_dynamic-update-slice_fusion.4
  165.1 1.3 bitcast_dynamic-update-slice_fusion.4
  166.4 19.7 %custom-call.14 = f32[2,128,128]{1,2,0:T(8,128)S(1)} custom-call(f32[2,128,128]{2,1,0:T(8,128)S(1)} %get-tuple-element.18), custom_call_target="InvertDiagBlocksLowerTriangular" | custom-call | tf_op jit(solution)/shard_map/jit(_solve_triangular)/triangular_solve | solution.py:25
  187.6 0.8 fusion.2
  188.5 52.6 %all-gather.5.cloned.1.call-done = f32[4096,256]{1,0:T(8,128)} async-done(((f32[512,256]{1,0:T(8,128)}), f32[4096,256]{1,0:T(8,128)}) %all-gather.5.cloned.1.call-update) | async-done | bytes 4194320 | tf_op jit(solution)/shard_map/all_gather | solution.py:16
  241.1 2.5 reduce_sum.18
  243.7 2.6 fusion.57
  246.4 193.7 %all-reduce.8.cloned.1.call-done = f32[256,512]{0,1:T(8,128)} async-done(((f32[256,512]{0,1:T(8,128)}), f32[256,512]{0,1:T(8,128)}) %all-reduce.8.cloned.1.call-update) | async-done | bytes 524304 | tf_op jit(solution)/shard_map/psum | solution.py:57
  440.1 2.2 fusion
  442.3 1.0 fusion.6
  443.3 1.9 collective-permute-start.6
  445.2 1.5 collective-permute-done.6
  446.8 3.1 collective-permute-start.7
  449.9 7.1 collective-permute-done.7
  457.0 4.4 collective-permute-start.8
  461.4 6.5 collective-permute-done.8
  468.0 1.9 collective-permute-start.9
  469.9 6.6 collective-permute-done.9
  476.5 3.4 collective-permute-start.10
  480.0 10.6 %collective-permute-done.10 = f32[256,256]{0,1:T(8,128)S(1)} collective-permute-done((f32[256,256]{0,1:T(8,128)S(1)}, f32[256,256]{0,1:T(8,128)S(1)}, u32[]{:S(2)}, u32[]{:S(2)}) %collective-permute-start.10) | collective-permute-done | bytes 262176 | tf_op jit(solution)/shard_map/ppermute | solution.py:11
  490.7 4.7 collective-permute-start.11
  495.5 13.5 %collective-permute-done.11 = f32[256,256]{0,1:T(8,128)S(1)} collective-permute-done((f32[256,256]{0,1:T(8,128)S(1)}, f32[256,256]{0,1:T(8,128)S(1)}, u32[]{:S(2)}, u32[]{:S(2)}) %collective-permute-start.11) | collective-permute-done | bytes 262176 | tf_op jit(solution)/shard_map/ppermute | solution.py:11
  509.2 11.7 %cholesky.164 = f32[128,128]{1,0:T(8,128)S(1)} custom-call(f32[128,128]{1,0:T(8,128)S(1)} %cholesky.197), custom_call_target="Cholesky" | custom-call | tf_op jit(solution)/shard_map/jit(cholesky)/cholesky | solution.py:24
  520.9 9.8 %custom-call.15 = f32[1,128,128]{1,2,0:T(8,128)S(1)} custom-call(f32[1,128,128]{2,1,0:T(8,128)S(1)} %get-tuple-element.53), custom_call_target="InvertDiagBlocksLowerTriangular" | custom-call | tf_op jit(solution)/shard_map/jit(cholesky)/cholesky | solution.py:24
  532.1 11.7 %cholesky.181 = f32[128,128]{1,0:T(8,128)S(1)} custom-call(f32[128,128]{1,0:T(8,128)S(1)} %slice_subtract_fusion), custom_call_target="Cholesky" | custom-call | tf_op jit(solution)/shard_map/jit(cholesky)/cholesky | solution.py:24
  545.9 4.1 while.5
  546.7 1.4 bitcast_dynamic-update-slice_fusion.5
  548.7 1.4 bitcast_dynamic-update-slice_fusion.5
  550.1 19.7 %custom-call.16 = f32[2,128,128]{1,2,0:T(8,128)S(1)} custom-call(f32[2,128,128]{2,1,0:T(8,128)S(1)} %get-tuple-element.19), custom_call_target="InvertDiagBlocksLowerTriangular" | custom-call | tf_op jit(solution)/shard_map/jit(_solve_triangular)/triangular_solve | solution.py:25
  571.3 0.8 fusion.3
  572.2 53.4 %all-gather.7.cloned.1.call-done = f32[4096,256]{1,0:T(8,128)} async-done(((f32[512,256]{1,0:T(8,128)}), f32[4096,256]{1,0:T(8,128)}) %all-gather.7.cloned.1.call-update) | async-done | bytes 4194320 | tf_op jit(solution)/shard_map/all_gather | solution.py:16
  625.6 2.5 reduce_sum.19
  628.1 2.6 fusion.58
  630.7 1.0 select_multiply_fusion.1
  631.7 0.8 broadcast_multiply_fusion
  632.6 192.0 %all-reduce.10.cloned.1.call-done = f32[256,512]{0,1:T(8,128)} async-done(((f32[256,512]{0,1:T(8,128)}), f32[256,512]{0,1:T(8,128)}) %all-reduce.10.cloned.1.call-update) | async-done | bytes 524304 | tf_op jit(solution)/shard_map/psum | solution.py:57
  824.6 1.3 select_multiply_fusion
  825.9 1.2 pad_maximum_fusion
  827.1 1.3 copy.54
  828.4 3.1 fusion.1
  (87 shorter events, 13.4 us)
Async XLA Ops:
  7.2 47.8 %copy-start = (f32[512,512]{1,0:T(8,128)S(1)}, f32[512,512]{1,0:T(8,128)}, u32[]{:S(2)}) copy-start(f32[512,512]{1,0:T(8,128)} %param.8) | copy-start | bytes 3145732
  7.2 29.5 %copy-start.3 = (s32[256]{0:T(256)S(1)}, s32[256]{0:T(256)}, u32[]{:S(2)}) copy-start(s32[256]{0:T(256)} %param.12) | copy-start | bytes 3076
  8.7 23.3 %all-to-all-start = ((s32[64,1,8]{2,1,0:T(1,128)}), s32[64,1,8]{2,1,0:T(1,128)S(1)}, u32[]{:S(2)}, u32[]{:S(2)}) async-start(s32[64,1,8]{2,1,0:T(1,128)} %bitcast), calls=%async_computation | async-start | bytes 65536 | tf_op jit(solution)/shard_map/all_to_all | solution.py:41
  32.0 22.3 %all-to-all-start.1 = ((f32[64,8,256]{2,1,0:T(8,128)}), f32[64,8,256]{2,1,0:T(8,128)S(1)}, u32[]{:S(2)}, u32[]{:S(2)}) async-start(f32[64,8,256]{2,1,0:T(8,128)} %bitcast_multiply_fusion), calls=%async_computation.1 | async-start | bytes 1048576 | tf_op jit(solution)/shard_map/all_to_all | solution.py:40
  36.6 204.5 %all-gather.5.cloned.1.call-start = ((), (), s32[]{:S(2)}) async-start(), calls=%async_computation.4 | async-start | bytes 4718592 | tf_op jit(solution)/shard_map/all_gather | solution.py:16
  60.0 3.4 collective-permute-start
  63.5 10.2 %collective-permute-start.1 = (f32[256,256]{0,1:T(8,128)S(1)}, f32[256,256]{0,1:T(8,128)S(1)}, u32[]{:S(2)}, u32[]{:S(2)}) collective-permute-start(f32[256,256]{0,1:T(8,128)S(1)} %add.121), channel_id=1, source_target_pairs={{0,16},{8,24},{16,0},{24,8},{32,48},{40,56},{48,32},{56,40},{64,80... | collective-permute-start | bytes 786440 | tf_op jit(solution)/shard_map/ppermute | solution.py:11
  73.7 10.9 %collective-permute-start.2 = (f32[256,256]{0,1:T(8,128)S(1)}, f32[256,256]{0,1:T(8,128)S(1)}, u32[]{:S(2)}, u32[]{:S(2)}) collective-permute-start(f32[256,256]{0,1:T(8,128)S(1)} %add.122), channel_id=1, source_target_pairs={{0,32},{8,40},{16,48},{24,56},{32,0},{40,8},{48,16},{56,24},{64,96... | collective-permute-start | bytes 786440 | tf_op jit(solution)/shard_map/ppermute | solution.py:11
  84.7 8.5 %collective-permute-start.3 = (f32[256,256]{0,1:T(8,128)S(1)}, f32[256,256]{0,1:T(8,128)S(1)}, u32[]{:S(2)}, u32[]{:S(2)}) collective-permute-start(f32[256,256]{0,1:T(8,128)S(1)} %add.123), channel_id=1, source_target_pairs={{0,64},{8,72},{16,80},{24,88},{32,96},{40,104},{48,112},{56,120},{... | collective-permute-start | bytes 786440 | tf_op jit(solution)/shard_map/ppermute | solution.py:11
  93.2 14.2 %collective-permute-start.4 = (f32[256,256]{0,1:T(8,128)S(1)}, f32[256,256]{0,1:T(8,128)S(1)}, u32[]{:S(2)}, u32[]{:S(2)}) collective-permute-start(f32[256,256]{0,1:T(8,128)S(1)} %add.124), channel_id=1, source_target_pairs={{0,128},{8,136},{16,144},{24,152},{32,160},{40,168},{48,176},{56,1... | collective-permute-start | bytes 786440 | tf_op jit(solution)/shard_map/ppermute | solution.py:11
  107.5 18.3 %collective-permute-start.5 = (f32[256,256]{0,1:T(8,128)S(1)}, f32[256,256]{0,1:T(8,128)S(1)}, u32[]{:S(2)}, u32[]{:S(2)}) collective-permute-start(f32[256,256]{0,1:T(8,128)S(1)} %add.125), channel_id=1, source_target_pairs={{0,256},{8,264},{16,272},{24,280},{32,288},{40,296},{48,304},{56,3... | collective-permute-start | bytes 786440 | tf_op jit(solution)/shard_map/ppermute | solution.py:11
  188.5 251.6 %all-reduce.8.cloned.1.call-start = ((), (), s32[]{:S(2)}) async-start(), calls=%async_computation.2 | async-start | bytes 1048576 | tf_op jit(solution)/shard_map/psum | solution.py:57
  246.3 379.3 %all-gather.7.cloned.1.call-start = ((), (), s32[]{:S(2)}) async-start(), calls=%async_computation.5 | async-start | bytes 4718592 | tf_op jit(solution)/shard_map/all_gather | solution.py:16
  443.3 3.4 collective-permute-start.6
  446.8 10.2 %collective-permute-start.7 = (f32[256,256]{0,1:T(8,128)S(1)}, f32[256,256]{0,1:T(8,128)S(1)}, u32[]{:S(2)}, u32[]{:S(2)}) collective-permute-start(f32[256,256]{0,1:T(8,128)S(1)} %add.127), channel_id=1, source_target_pairs={{0,16},{8,24},{16,0},{24,8},{32,48},{40,56},{48,32},{56,40},{64,80... | collective-permute-start | bytes 786440 | tf_op jit(solution)/shard_map/ppermute | solution.py:11
  457.0 10.9 %collective-permute-start.8 = (f32[256,256]{0,1:T(8,128)S(1)}, f32[256,256]{0,1:T(8,128)S(1)}, u32[]{:S(2)}, u32[]{:S(2)}) collective-permute-start(f32[256,256]{0,1:T(8,128)S(1)} %add.128), channel_id=1, source_target_pairs={{0,32},{8,40},{16,48},{24,56},{32,0},{40,8},{48,16},{56,24},{64,96... | collective-permute-start | bytes 786440 | tf_op jit(solution)/shard_map/ppermute | solution.py:11
  468.0 8.5 %collective-permute-start.9 = (f32[256,256]{0,1:T(8,128)S(1)}, f32[256,256]{0,1:T(8,128)S(1)}, u32[]{:S(2)}, u32[]{:S(2)}) collective-permute-start(f32[256,256]{0,1:T(8,128)S(1)} %add.129), channel_id=1, source_target_pairs={{0,64},{8,72},{16,80},{24,88},{32,96},{40,104},{48,112},{56,120},{... | collective-permute-start | bytes 786440 | tf_op jit(solution)/shard_map/ppermute | solution.py:11
  476.5 14.1 %collective-permute-start.10 = (f32[256,256]{0,1:T(8,128)S(1)}, f32[256,256]{0,1:T(8,128)S(1)}, u32[]{:S(2)}, u32[]{:S(2)}) collective-permute-start(f32[256,256]{0,1:T(8,128)S(1)} %add.130), channel_id=1, source_target_pairs={{0,128},{8,136},{16,144},{24,152},{32,160},{40,168},{48,176},{56,1... | collective-permute-start | bytes 786440 | tf_op jit(solution)/shard_map/ppermute | solution.py:11
  490.7 18.3 %collective-permute-start.11 = (f32[256,256]{0,1:T(8,128)S(1)}, f32[256,256]{0,1:T(8,128)S(1)}, u32[]{:S(2)}, u32[]{:S(2)}) collective-permute-start(f32[256,256]{0,1:T(8,128)S(1)} %add.131), channel_id=1, source_target_pairs={{0,256},{8,264},{16,272},{24,280},{32,288},{40,296},{48,304},{56,3... | collective-permute-start | bytes 786440 | tf_op jit(solution)/shard_map/ppermute | solution.py:11
  572.1 58.6 %copy-start.1 = (f32[256,512]{0,1:T(8,128)S(1)}, f32[256,512]{0,1:T(8,128)}, u32[]{:S(2)}) copy-start(f32[256,512]{0,1:T(8,128)} %all-reduce.8.cloned.1.call-done) | copy-start | bytes 1572868
  572.1 252.4 %all-reduce.10.cloned.1.call-start = ((), (), s32[]{:S(2)}) async-start(), calls=%async_computation.3 | async-start | bytes 1048576 | tf_op jit(solution)/shard_map/psum | solution.py:57
  824.6 3.8 copy-start.2
Sparse Core Ops, SparseCore 0:
  188.6 52.5 all-gather.4
  246.4 193.6 all-reduce.7
  572.3 53.2 all-gather.6
  630.8 193.6 all-reduce.9
